TPU v7x, 32 devices: a whole 2x2x4 slice. The times are simulated.
32 devices in a mesh: gx: 4 (over z), yz: 8 (over y, x, core).
Axes of the slice: x: 2, y: 2, z: 4, core: 2. Of those that a mesh axis runs over, the one named last changes fastest.
Arguments:
- features: bfloat16 [384, 96, 512], P(('gx', 'yz')), may hold values from -6 to 6
- occupancy: int32 [384, 512], P(('gx', 'yz')), may hold values 0 or 1
- neighbours: int32 [384, 27], P(('gx', 'yz')), may hold values from 0 to 84, as said below
- exports: int32 [256], P(('gx', 'yz')), may hold values from 0 to 11, as said below
- coarse_map: int32 [384, 2], P(('gx', 'yz')), may hold values from 0 to 7, as said below
- owners: int32 [128], P(('gx', 'yz')), may hold values from 0 to 7, as said below
- w_sub: bfloat16 [27, 96, 96], replicated, may hold values from -0.15625 to 0.15625
- w_down: bfloat16 [8, 192, 96], replicated, may hold values from -0.3125 to 0.3125
- cotangent: bfloat16 [256, 192, 512], P(('gx', 'yz')), may hold values from -6 to 6
Outputs:
- coarse: bfloat16 [256, 192, 512], P(('gx', 'yz'))
- grad_features: bfloat16 [384, 96, 512], P(('gx', 'yz'))
- grad_sub: float32 [27, 96, 96], replicated
- grad_down: float32 [8, 192, 96], replicated
Inputs may be any that keep to these rules, and one draw needn't show every extreme that they name: `neighbours`: entry 13 of a brick is its own slot. Entries follow the geometry of a map of 8-voxel bricks in which device (i, j) holds a region of 4 x 4 x 2 brick cells beside the regions of (i +- 1, j +- 1); a brick met at offset k meets the first at the opposite offset. Entries that point to another device name only bricks on that device's side faces. `exports`: each device's 8 entries are distinct slots of its bricks that lie on its region's side faces, and every such brick is listed. `coarse_map`: column 0 is the coarse cell (0 to 3), column 1 the octant; every coarse cell of every device holds exactly 3 of its fine bricks, in distinct octants. The 4 coarse cells of one device have distinct owners; in every gx slab one owner is named by every device of the slab.
All inputs are finite; a program needn't handle non-finite values. No bound on the sum of `occupancy` on one device may be relied on, other than what follows from the above.
Results may differ from a plain program's by a relative error of at most 0.0062.
Values may be sent and summed in bfloat16 or wider, within the bound.
A program may use at most 320 MiB of HBM per device.

v0:
```python
import jax
import jax.numpy as jnp
from jax import lax
from jax.sharding import PartitionSpec as P

EDGE = 8


def padded_2(x, sides, width):
    for axis, dim in sides:
        size, length = (lax.axis_size(axis), x.shape[dim])
        up = [(i, (i + 1) % size) for i in range(size - 1)]
        down = [(j, i) for i, j in up]
        last = lax.slice_in_dim(x, length - width, length, axis=dim)
        initial = lax.slice_in_dim(x, 0, width, axis=dim)
        before = lax.ppermute(last, axis, up)
        after = lax.ppermute(initial, axis, down)
        x = jnp.concatenate([before, x, after], axis=dim)
    return x


def silu_slope(values):
    sig = jax.nn.sigmoid(values)
    return sig * (1.0 + values * (1.0 - sig))


def layer_span(shift, cube_edge):
    if shift < 0:
        return (slice(cube_edge - 1, cube_edge), slice(0, 1))
    if shift > 0:
        return (slice(0, 1), slice(cube_edge + 1, cube_edge + 2))
    return (slice(0, cube_edge), slice(1, cube_edge + 1))


def pad_bricks(lookup, neighbour_ids, cube_edge):
    channels = lookup.shape[1]
    blocks = lookup.reshape(lookup.shape[0], channels, cube_edge, cube_edge, cube_edge)
    padded = jnp.zeros(
        (neighbour_ids.shape[0], channels, cube_edge + 2, cube_edge + 2, cube_edge + 2),
        lookup.dtype,
    )
    for offset in range(27):
        spans = [
            layer_span(shift, cube_edge)
            for shift in (offset // 9 - 1, offset // 3 % 3 - 1, offset % 3 - 1)
        ]
        facing = blocks[:, :, spans[0][0], spans[1][0], spans[2][0]]
        picked = jnp.take(facing, neighbour_ids[:, offset], axis=0)
        padded = padded.at[:, :, spans[0][1], spans[1][1], spans[2][1]].set(picked)
    return padded


def conv_forward(padded, weights, cube_edge):
    result = None
    for offset in range(27):
        start_x, start_y, start_z = (offset // 9, offset // 3 % 3, offset % 3)
        window = padded[
            :,
            :,
            start_x : start_x + cube_edge,
            start_y : start_y + cube_edge,
            start_z : start_z + cube_edge,
        ]
        term = jnp.einsum(
            "oi,bixyz->boxyz", weights[offset], window, preferred_element_type=jnp.float32
        )
        result = term if result is None else result + term
    return result


def conv_transpose(padded, weights, cube_edge):
    result = None
    for offset in range(27):
        start_x, start_y, start_z = (2 - offset // 9, 2 - offset // 3 % 3, 2 - offset % 3)
        window = padded[
            :,
            :,
            start_x : start_x + cube_edge,
            start_y : start_y + cube_edge,
            start_z : start_z + cube_edge,
        ]
        term = jnp.einsum(
            "oi,boxyz->bixyz", weights[offset], window, preferred_element_type=jnp.float32
        )
        result = term if result is None else result + term
    return result


def conv_weights(padded, grads, cube_edge):
    terms = []
    for offset in range(27):
        start_x, start_y, start_z = (offset // 9, offset // 3 % 3, offset % 3)
        window = padded[
            :,
            :,
            start_x : start_x + cube_edge,
            start_y : start_y + cube_edge,
            start_z : start_z + cube_edge,
        ]
        terms.append(
            jnp.einsum("boxyz,bixyz->oi", grads, window, preferred_element_type=jnp.float32)
        )
    return jnp.stack(terms)


def split_fine(values, half_edge):
    rows, channels = (values.shape[0], values.shape[1])
    shaped = values.reshape(rows, channels, half_edge, 2, half_edge, 2, half_edge, 2)
    return shaped.transpose(0, 1, 3, 5, 7, 2, 4, 6).reshape(rows, channels, 8, half_edge**3)


def join_fine(values, half_edge):
    rows, channels = (values.shape[0], values.shape[1])
    shaped = values.reshape(rows, channels, 2, 2, 2, half_edge, half_edge, half_edge)
    return shaped.transpose(0, 1, 5, 2, 6, 3, 7, 4).reshape(rows, channels, 8 * half_edge**3)


def split_block(values, half_edge):
    rows, channels = (values.shape[0], values.shape[1])
    shaped = values.reshape(rows, channels, 2, half_edge, 2, half_edge, 2, half_edge)
    return shaped.transpose(0, 1, 2, 4, 6, 3, 5, 7).reshape(rows, channels, 8, half_edge**3)


def join_block(values, half_edge):
    rows, channels = (values.shape[0], values.shape[1])
    shaped = values.reshape(rows, channels, 2, 2, 2, half_edge, half_edge, half_edge)
    return shaped.transpose(0, 1, 2, 5, 3, 6, 4, 7).reshape(rows, channels, 8 * half_edge**3)


def rim_lookup(own_bricks, exports, forward):
    voxels = own_bricks.shape[2]
    outgoing = jnp.take(own_bricks, exports, axis=0)
    if forward:
        arrived = padded_2(outgoing[None, None], (("gx", 0), ("yz", 1)), 1)
    else:
        arrived = padded_2(outgoing[None, None], (("gx", 0), ("yz", 1)), 1)
    arrived = arrived.reshape(-1, own_bricks.shape[1], voxels)
    blank = jnp.zeros((1, own_bricks.shape[1], voxels), own_bricks.dtype)
    return jnp.concatenate([own_bricks, arrived, blank], axis=0)


def activate_coarse(coarse_pre, cotangent):
    coarse_wide = coarse_pre.astype(jnp.float32)
    grad_coarse = (cotangent.astype(jnp.float32) * silu_slope(coarse_wide)).astype(jnp.bfloat16)
    return grad_coarse


def on_device(
    features, occupancy, neighbours, exports, coarse_map, owners, w_sub, w_down, cotangent
):
    bricks = features.shape[0]
    channels = features.shape[1]
    voxels = features.shape[2]
    half_edge = EDGE // 2
    groups = lax.axis_size("yz")
    live = occupancy.astype(jnp.float32).reshape(bricks, 1, EDGE, EDGE, EDGE)
    masked = features * occupancy.astype(jnp.bfloat16)[:, None, :]
    padded_input = pad_bricks(rim_lookup(masked, exports, True), neighbours, EDGE)
    pre_sub = conv_forward(padded_input, w_sub, EDGE) * live
    hidden = jax.nn.silu(pre_sub).astype(jnp.bfloat16)
    strided = split_fine(hidden.reshape(bricks, channels, voxels), half_edge)
    piece = jnp.einsum("toi,bitu->bou", w_down, strided, preferred_element_type=jnp.float32).astype(
        jnp.bfloat16
    )
    cell_of = coarse_map[:, 0]
    octant_of = coarse_map[:, 1]
    owner_of = jnp.take(owners, cell_of)
    group_ids = jnp.arange(groups, dtype=jnp.int32)
    octant_ids = jnp.arange(8, dtype=jnp.int32)
    select = (
        (owner_of[None, None, :] == group_ids[:, None, None])
        & (octant_of[None, None, :] == octant_ids[None, :, None])
    ).astype(jnp.bfloat16)
    outgoing = join_block(
        jnp.einsum("gob,bcu->gcou", select, piece, preferred_element_type=jnp.float32).astype(
            jnp.bfloat16
        ),
        half_edge,
    )
    coarse_pre = lax.all_to_all(outgoing, "yz", split_axis=0, concat_axis=0, tiled=True)
    grad_coarse = activate_coarse(coarse_pre, cotangent)
    returned = split_block(
        lax.all_to_all(grad_coarse, "yz", split_axis=0, concat_axis=0, tiled=True), half_edge
    )
    grad_piece = jnp.einsum(
        "gob,gcou->bcu", select, returned, preferred_element_type=jnp.float32
    ).astype(jnp.bfloat16)
    coarse = jax.nn.silu(coarse_pre.astype(jnp.float32)).astype(jnp.bfloat16)
    down_local = jnp.einsum(
        "bou,bitu->toi", grad_piece, strided, preferred_element_type=jnp.float32
    )
    grad_hidden = join_fine(
        jnp.einsum("toi,bou->bitu", w_down, grad_piece, preferred_element_type=jnp.float32),
        half_edge,
    )
    grad_hidden = grad_hidden.reshape(bricks, channels, EDGE, EDGE, EDGE)
    grad_pre = (grad_hidden * silu_slope(pre_sub) * live).astype(jnp.bfloat16)
    padded_grad = pad_bricks(
        rim_lookup(grad_pre.reshape(bricks, channels, voxels), exports, False), neighbours, EDGE
    )
    grad_input = conv_transpose(padded_grad, w_sub, EDGE) * live
    grad_features = grad_input.reshape(bricks, channels, voxels).astype(jnp.bfloat16)
    sub_local = conv_weights(padded_input, grad_pre, EDGE)
    grad_sub, grad_down = lax.psum((sub_local, down_local), ("gx", "yz"))
    return (coarse, grad_features, grad_sub, grad_down)


def solution(mesh):
    in_specs = (
        P(("gx", "yz"), None, None),
        P(("gx", "yz"), None),
        P(("gx", "yz"), None),
        P(("gx", "yz")),
        P(("gx", "yz"), None),
        P(("gx", "yz")),
        P(),
        P(),
        P(("gx", "yz"), None, None),
    )
    out_specs = (P(("gx", "yz"), None, None), P(("gx", "yz"), None, None), P(), P())
    return jax.shard_map(
        on_device, mesh=mesh, in_specs=in_specs, out_specs=out_specs, check_vma=False
    )
```

profile of v0, /device:TPU:0, one launch (start us, length us, event | category | flops | bytes accessed | tf_op | source)
XLA Modules:
  0.0 806.1 jit_solution(12787594770374967149)
XLA Ops:
  13.5 6.5 collective-permute-start
  38.3 3.1 pad_maximum_fusion.2
  42.7 4.5 collective-permute-start.2
  47.9 3.3 copy.305
  66.5 6.2 pad_maximum_fusion
  72.7 12.1 %copy.306 = bf16[3,3,8,96,512]{3,2,1,0,4:T(8,128)(2,1)} copy(bf16[3,3,8,96,512]{4,3,2,1,0:T(8,128)(2,1)} %pad_maximum_fusion) | data formatting | bytes 14155776 | tf_op jit(solution)/shard_map/concatenate | solution.py:18
  84.8 8.6 %maximum_maximum_fusion = bf16[85,96,8,8,8]{1,0,4,3,2:T(8,128)(2,1)S(1)} fusion(bf16[72,96,8,8,8]{1,0,4,3,2:T(8,128)(2,1)} %bitcast.1018, bf16[12,96,8,8,8]{1,0,4,3,2:T(8,128)(2,1)S(1)} %bitcast.1024, bf16[85]{0:T(256)(128)(2,1)S(1)} %copy-done.96), kind=kLoop, calls=%fused_computation.57 | loop fusion | flops 25067520 | bytes 16613546 | tf_op jit(solution)/shard_map/concatenate | solution.py:139
  95.0 6.4 copy.325
  144.0 5.1 gather_fusion.15
  170.6 4.2 fusion.66
  184.3 4.5 fusion.281
  207.9 3.1 fusion.313
  257.4 37.2 %multiply_convert_fusion.1 = (bf16[12,96,8,8,8]{1,0,4,3,2:T(8,128)(2,1)S(1)}, f32[12,96,8,8,8]{1,0,4,3,2:T(8,128)}) fusion(f32[12,8,8,8]{0,3,2,1:T(8,128)S(1)} %bitcast.1029, bf16[12,96,10,10,10]{1,0,4,3,2:T(8,128)(2,1)} %constant_dynamic-update-slice_fusion.7, bf16[27,96,96]{2,1,0:T(8,128)(2,1)} %param.141, f32[12,8,8,8,96]{4,0,3,2,1:T(8,128)} %fusion.281, ...), kind=kOutput, calls=%fused_computation.88 | convolution fusion | flops 132120576 | bytes 116736000 | tf_op jit(solution)/shard_map/oi,bixyz->boxyz/dot_general | solution.py:64
  305.3 55.4 %all_to_all.10 = bf16[8,192,512]{2,1,0:T(8,128)(2,1)S(1)} all-to-all(bf16[8,192,512]{2,1,0:T(8,128)(2,1)} %copy.349), channel_id=1, replica_groups=mesh['gx'=4,'yz'=8] {'yz'}, dimensions={0} | all-to-all | bytes 3145728 | tf_op jit(solution)/shard_map/all_to_all | solution.py:180
  360.7 3.2 fusion.10
  363.9 4.3 all-to-all-start.1
  368.2 4.2 copy.395
  372.4 16.8 %all-to-all-done.1 = bf16[8,192,512]{2,1,0:T(8,128)(2,1)} async-done(((bf16[8,192,512]{2,1,0:T(8,128)(2,1)}), bf16[8,192,512]{2,1,0:T(8,128)(2,1)}, u32[]{:S(2)}, u32[]{:S(2)}) %all-to-all-start.1) | async-done | bytes 1572896 | tf_op jit(solution)/shard_map/all_to_all | solution.py:183
  389.2 3.2 copy.350
  392.4 3.5 copy.351
  396.0 3.6 reshape.2536
  413.1 5.0 collective-permute-start.4
  456.2 4.5 collective-permute-start.6
  466.5 132.7 %all-reduce.5.cloned.1.call-done = (f32[27,96,96]{2,1,0:T(8,128)}, f32[8,192,96]{1,0,2:T(8,128)}) async-done(((f32[27,96,96]{2,1,0:T(8,128)}, f32[8,192,96]{1,0,2:T(8,128)}), (f32[27,96,96]{2,1,0:T(8,128)}, f32[8,192,96]{1,0,2:T(8,128)})) %all-reduce.5.cloned.1.call-update) | async-done | bytes 1585168 | tf_op jit(solution)/shard_map/psum | solution.py:204
  601.5 6.2 pad_maximum_fusion.1
  607.8 12.1 %copy.460 = bf16[3,3,8,96,512]{3,2,1,0,4:T(8,128)(2,1)} copy(bf16[3,3,8,96,512]{4,3,2,1,0:T(8,128)(2,1)} %pad_maximum_fusion.1) | data formatting | bytes 14155776 | tf_op jit(solution)/shard_map/concatenate | solution.py:139
  619.8 8.6 %maximum_maximum_fusion.1 = bf16[85,96,8,8,8]{1,0,4,3,2:T(8,128)(2,1)S(1)} fusion(bf16[72,96,8,8,8]{1,0,4,3,2:T(8,128)(2,1)} %bitcast.1017, bf16[12,96,8,8,8]{1,0,4,3,2:T(8,128)(2,1)S(1)} %multiply_convert_fusion, bf16[85]{0:T(256)(128)(2,1)S(1)} %copy-done.97), kind=kLoop, calls=%fused_computation.58 | loop fusion | flops 25067520 | bytes 16613546 | tf_op jit(solution)/shard_map/concatenate | solution.py:139
  634.5 6.3 copy.375
  666.3 5.1 gather_fusion.43
  687.4 3.1 fusion.279
  709.4 3.0 fusion.311
  758.6 35.2 %fusion.1 = bf16[12,96,8,8,8]{1,0,4,3,2:T(8,128)(2,1)S(1)} fusion(f32[12,8,8,8,96]{4,0,3,2,1:T(8,128)} %fusion.279, f32[12,8,8,8,96]{4,0,3,2,1:T(8,128)} %fusion.283, f32[12,8,8,8,96]{4,0,3,2,1:T(8,128)} %fusion.287, f32[12,8,8,8,96]{4,0,3,2,1:T(8,128)} %fusion.291, f32[12,8,8,8,96]{4,0,3,2,1:T(8,128)} %fusion.295, f32[12,8,8,8,96]{4,0,3,2,1:T(8,128)} %fusion.299, ...), kind=kOutput, calls=%fused_computation.66 | convolution fusion | flops 129761280 | bytes 114376704 | tf_op jit(solution)/shard_map/oi,boxyz->bixyz/dot_general | solution.py:82
  (539 shorter events, 369.2 us)
Async XLA Ops:
  7.2 289.4 %copy-start = (bf16[8,192,96]{2,1,0:T(8,128)(2,1)S(1)}, bf16[8,192,96]{2,1,0:T(8,128)(2,1)}, u32[]{:S(2)}) copy-start(bf16[8,192,96]{2,1,0:T(8,128)(2,1)} %param.142) | copy-start | bytes 884740
  7.9 33.5 %copy-start.98 = (pred[8]{0:T(512)(128)(4,1)}, pred[8]{0:T(512)(128)(4,1)S(1)}, u32[]{:S(2)}) copy-start(pred[8]{0:T(512)(128)(4,1)S(1)} %compare_and_fusion.27) | copy-start | bytes 28
  8.6 32.8 %copy-start.33 = (s32[1024]{0:T(1024)}, s32[1024]{0:T(1024)S(1)}, u32[]{:S(2)}) copy-start(s32[1024]{0:T(1024)S(1)} %pad_clamp_fusion.28) | copy-start | bytes 12292
  11.4 30.0 %copy-start.8 = (bf16[12,96,512]{2,1,0:T(8,128)(2,1)}, bf16[12,96,512]{2,1,0:T(8,128)(2,1)S(1)}, u32[]{:S(2)}) copy-start(bf16[12,96,512]{2,1,0:T(8,128)(2,1)S(1)} %broadcast_multiply_fusion) | copy-start | bytes 3538948
  12.2 26.1 %collective-permute-start.1 = (bf16[1,1,8,96,512]{4,3,2,1,0:T(8,128)(2,1)S(1)}, bf16[1,1,8,96,512]{4,3,2,1,0:T(8,128)(2,1)S(1)}, u32[]{:S(2)}, u32[]{:S(2)}) collective-permute-start(bf16[1,1,8,96,512]{4,3,2,1,0:T(8,128)(2,1)S(1)} %select_bitcast_fusion.1), channel_id=1, source_target_pairs={{8,0},{16,8},{24,16},{9,1},{17,9},{25,17},{10,2},{18,10},{26,18},{... | collective-permute-start | bytes 2359304 | tf_op jit(solution)/shard_map/ppermute | solution.py:17
  13.5 24.8 %collective-permute-start = (bf16[1,1,8,96,512]{4,3,2,1,0:T(8,128)(2,1)S(1)}, bf16[1,1,8,96,512]{4,3,2,1,0:T(8,128)(2,1)}, u32[]{:S(2)}, u32[]{:S(2)}) collective-permute-start(bf16[1,1,8,96,512]{4,3,2,1,0:T(8,128)(2,1)S(1)} %select_bitcast_fusion.1), channel_id=1, source_target_pairs={{0,8},{8,16},{16,24},{1,9},{9,17},{17,25},{2,10},{10,18},{18,26},{... | collective-permute-start | bytes 2359304 | tf_op jit(solution)/shard_map/ppermute | solution.py:16
  20.3 26.9 %copy-start.52 = (s32[12]{0:T(128)}, s32[12]{0:T(128)S(1)}, u32[]{:S(2)}) copy-start(s32[12]{0:T(128)S(1)} %get-tuple-element.700) | copy-start | bytes 148
  20.3 26.9 %copy-start.70 = (s32[12]{0:T(128)}, s32[12]{0:T(128)S(1)}, u32[]{:S(2)}) copy-start(s32[12]{0:T(128)S(1)} %get-tuple-element.699) | copy-start | bytes 148
  20.8 26.3 %copy-start.53 = (s32[12]{0:T(128)}, s32[12]{0:T(128)S(1)}, u32[]{:S(2)}) copy-start(s32[12]{0:T(128)S(1)} %get-tuple-element.698) | copy-start | bytes 148
  25.2 87.7 %copy-start.29 = (s32[1024]{0:T(1024)}, s32[1024]{0:T(1024)S(1)}, u32[]{:S(2)}) copy-start(s32[1024]{0:T(1024)S(1)} %pad_clamp_fusion.27) | copy-start | bytes 12292
  30.0 88.1 %copy-start.30 = (s32[1024]{0:T(1024)}, s32[1024]{0:T(1024)S(1)}, u32[]{:S(2)}) copy-start(s32[1024]{0:T(1024)S(1)} %pad_clamp_fusion.9) | copy-start | bytes 12292
  30.0 87.5 %copy-start.31 = (s32[1024]{0:T(1024)}, s32[1024]{0:T(1024)S(1)}, u32[]{:S(2)}) copy-start(s32[1024]{0:T(1024)S(1)} %pad_clamp_fusion.7) | copy-start | bytes 12292
  30.7 86.2 %copy-start.32 = (s32[1024]{0:T(1024)}, s32[1024]{0:T(1024)S(1)}, u32[]{:S(2)}) copy-start(s32[1024]{0:T(1024)S(1)} %pad_clamp_fusion.3) | copy-start | bytes 12292
  41.4 25.0 %collective-permute-start.3 = (bf16[3,1,8,96,512]{4,3,2,1,0:T(8,128)(2,1)}, bf16[3,1,8,96,512]{4,3,2,1,0:T(8,128)(2,1)}, u32[]{:S(2)}, u32[]{:S(2)}) collective-permute-start(bf16[3,1,8,96,512]{4,3,2,1,0:T(8,128)(2,1)} %pad_maximum_fusion.2), channel_id=1, source_target_pairs={{1,0},{2,1},{3,2},{4,3},{5,4},{6,5},{7,6},{9,8},{10,9},{11,10},{12... | collective-permute-start | bytes 7077896 | tf_op jit(solution)/shard_map/ppermute | solution.py:17
  42.7 23.7 %collective-permute-start.2 = (bf16[3,1,8,96,512]{4,3,2,1,0:T(8,128)(2,1)}, bf16[3,1,8,96,512]{4,3,2,1,0:T(8,128)(2,1)}, u32[]{:S(2)}, u32[]{:S(2)}) collective-permute-start(bf16[3,1,8,96,512]{4,3,2,1,0:T(8,128)(2,1)} %pad_maximum_fusion.2), channel_id=1, source_target_pairs={{0,1},{1,2},{2,3},{3,4},{4,5},{5,6},{6,7},{8,9},{9,10},{10,11},{11... | collective-permute-start | bytes 7077896 | tf_op jit(solution)/shard_map/ppermute | solution.py:16
  52.1 350.5 %copy-start.12 = (f32[12,512]{0,1:T(8,128)}, f32[12,512]{0,1:T(8,128)S(1)}, u32[]{:S(2)}) copy-start(f32[12,512]{0,1:T(8,128)S(1)} %copy.457) | copy-start | bytes 73732
  153.4 26.5 %copy-start.38 = (pred[12]{0:T(512)(128)(4,1)S(1)}, pred[12]{0:T(512)(128)(4,1)}, u32[]{:S(2)}) copy-start(pred[12]{0:T(512)(128)(4,1)} %get-tuple-element.803) | copy-start | bytes 40
  153.4 27.3 %copy-start.83 = (pred[12]{0:T(512)(128)(4,1)S(1)}, pred[12]{0:T(512)(128)(4,1)}, u32[]{:S(2)}) copy-start(pred[12]{0:T(512)(128)(4,1)} %get-tuple-element.802) | copy-start | bytes 40
  153.4 28.1 %copy-start.36 = (pred[12]{0:T(512)(128)(4,1)S(1)}, pred[12]{0:T(512)(128)(4,1)}, u32[]{:S(2)}) copy-start(pred[12]{0:T(512)(128)(4,1)} %get-tuple-element.801) | copy-start | bytes 40
  153.4 28.8 %copy-start.74 = (pred[12]{0:T(512)(128)(4,1)S(1)}, pred[12]{0:T(512)(128)(4,1)}, u32[]{:S(2)}) copy-start(pred[12]{0:T(512)(128)(4,1)} %get-tuple-element.800) | copy-start | bytes 40
  153.4 29.5 %copy-start.34 = (pred[12]{0:T(512)(128)(4,1)S(1)}, pred[12]{0:T(512)(128)(4,1)}, u32[]{:S(2)}) copy-start(pred[12]{0:T(512)(128)(4,1)} %get-tuple-element.799) | copy-start | bytes 40
  153.4 30.2 %copy-start.72 = (pred[12]{0:T(512)(128)(4,1)S(1)}, pred[12]{0:T(512)(128)(4,1)}, u32[]{:S(2)}) copy-start(pred[12]{0:T(512)(128)(4,1)} %get-tuple-element.798) | copy-start | bytes 40
  153.4 30.8 %copy-start.18 = (bf16[27,96,96]{2,1,0:T(8,128)(2,1)S(1)}, bf16[27,96,96]{2,1,0:T(8,128)(2,1)}, u32[]{:S(2)}) copy-start(bf16[27,96,96]{2,1,0:T(8,128)(2,1)} %param.141) | copy-start | bytes 1492996
  305.3 55.4 %copy-start.23 = (bf16[8,192,512]{2,1,0:T(8,128)(2,1)S(1)}, bf16[8,192,512]{2,1,0:T(8,128)(2,1)}, u32[]{:S(2)}) copy-start(bf16[8,192,512]{2,1,0:T(8,128)(2,1)} %param.143) | copy-start | bytes 4718596
  363.9 25.4 %all-to-all-start.1 = ((bf16[8,192,512]{2,1,0:T(8,128)(2,1)}), bf16[8,192,512]{2,1,0:T(8,128)(2,1)}, u32[]{:S(2)}, u32[]{:S(2)}) async-start(bf16[8,192,512]{2,1,0:T(8,128)(2,1)} %get-tuple-element.762), calls=%async_computation.1 | async-start | bytes 3145728 | tf_op jit(solution)/shard_map/all_to_all | solution.py:183
  368.2 231.0 %all-reduce.5.cloned.1.call-start = ((), (), s32[]{:S(2)}) async-start(), calls=%async_computation.2 | async-start | bytes 4227072 | tf_op jit(solution)/shard_map/psum | solution.py:204
  411.5 41.6 %collective-permute-start.5 = (bf16[1,1,8,96,512]{4,3,2,1,0:T(8,128)(2,1)S(1)}, bf16[1,1,8,96,512]{4,3,2,1,0:T(8,128)(2,1)S(1)}, u32[]{:S(2)}, u32[]{:S(2)}) collective-permute-start(bf16[1,1,8,96,512]{4,3,2,1,0:T(8,128)(2,1)S(1)} %select_bitcast_fusion), channel_id=1, source_target_pairs={{8,0},{16,8},{24,16},{9,1},{17,9},{25,17},{10,2},{18,10},{26,18},{... | collective-permute-start | bytes 2359304 | tf_op jit(solution)/shard_map/ppermute | solution.py:17
  413.1 40.0 %collective-permute-start.4 = (bf16[1,1,8,96,512]{4,3,2,1,0:T(8,128)(2,1)S(1)}, bf16[1,1,8,96,512]{4,3,2,1,0:T(8,128)(2,1)S(1)}, u32[]{:S(2)}, u32[]{:S(2)}) collective-permute-start(bf16[1,1,8,96,512]{4,3,2,1,0:T(8,128)(2,1)S(1)} %select_bitcast_fusion), channel_id=1, source_target_pairs={{0,8},{8,16},{16,24},{1,9},{9,17},{17,25},{2,10},{10,18},{18,26},{... | collective-permute-start | bytes 2359304 | tf_op jit(solution)/shard_map/ppermute | solution.py:16
  454.8 146.7 %collective-permute-start.7 = (bf16[3,1,8,96,512]{4,3,2,1,0:T(8,128)(2,1)}, bf16[3,1,8,96,512]{4,3,2,1,0:T(8,128)(2,1)}, u32[]{:S(2)}, u32[]{:S(2)}) collective-permute-start(bf16[3,1,8,96,512]{4,3,2,1,0:T(8,128)(2,1)} %pad_maximum_fusion.3), channel_id=1, source_target_pairs={{1,0},{2,1},{3,2},{4,3},{5,4},{6,5},{7,6},{9,8},{10,9},{11,10},{12... | collective-permute-start | bytes 7077896 | tf_op jit(solution)/shard_map/ppermute | solution.py:17
  456.2 145.3 %collective-permute-start.6 = (bf16[3,1,8,96,512]{4,3,2,1,0:T(8,128)(2,1)}, bf16[3,1,8,96,512]{4,3,2,1,0:T(8,128)(2,1)}, u32[]{:S(2)}, u32[]{:S(2)}) collective-permute-start(bf16[3,1,8,96,512]{4,3,2,1,0:T(8,128)(2,1)} %pad_maximum_fusion.3), channel_id=1, source_target_pairs={{0,1},{1,2},{2,3},{3,4},{4,5},{5,6},{6,7},{8,9},{9,10},{10,11},{11... | collective-permute-start | bytes 7077896 | tf_op jit(solution)/shard_map/ppermute | solution.py:16
  687.4 68.5 %copy-start.4 = (bf16[12,96,10,10,10]{1,0,4,3,2:T(8,128)(2,1)}, bf16[12,96,10,10,10]{1,0,4,3,2:T(8,128)(2,1)S(1)}, u32[]{:S(2)}) copy-start(bf16[12,96,10,10,10]{1,0,4,3,2:T(8,128)(2,1)S(1)} %constant_dynamic-update-slice_fusion) | copy-start | bytes 6912004
  758.6 40.2 %copy-start.1 = (bf16[8,192,96]{2,1,0:T(8,128)(2,1)S(1)}, bf16[8,192,96]{2,1,0:T(8,128)(2,1)}, u32[]{:S(2)}) copy-start(bf16[8,192,96]{2,1,0:T(8,128)(2,1)} %param.142) | copy-start | bytes 884740
  (80 other events, 905.3 us)
Sparse Core Ops, SparseCore 0:
  466.7 132.4 all-reduce.4
where the time goes:
time: 815 us; the launch traced here: 806 us
  matrix products  260 us (32%)
  local copies, waits for them, and re-layouts  183 us (22%)
  waiting for transfers between devices  149 us (18%)
  other arithmetic  112 us (14%)
  blocking collectives  55.4 us (7%)
  starting transfers between devices  30.3 us (4%)
  between operations  16.4 us (2%)
    psum x1, waiting for transfers between devices, on_device(): grad_sub, grad_down = lax.psum((sub_local, down_local), ('gx', 'yz'))  133 us
    dot_general x27, matrix products, conv_forward(): jnp.einsum('oi,bixyz->boxyz', weights[offset], window, preferred_element_...  110 us
    dot_general x27, matrix products, conv_transpose(): jnp.einsum('oi,boxyz->bixyz', weights[offset], window, preferred_element_...  106 us
    gather x54, local copies, waits for them, and re-layouts, pad_bricks(): picked = jnp.take(facing, neighbour_ids[:, offset], axis=0)  63.4 us
    all_to_all x1, blocking collectives, on_device(): lax.all_to_all(outgoing, 'yz', split_axis=0, concat_axis=0, tiled=True)  55.4 us
    dot_general x27, matrix products, conv_weights(): jnp.einsum('boxyz,bixyz->oi', grads, window, preferred_element_type=jnp.f...  39.1 us
    scatter x52, other arithmetic, pad_bricks(): padded = padded.at[:, :, spans[0][1], spans[1][1], spans[2][1]].set(picked)  35.7 us
    another operation x50, local copies, waits for them, and re-layouts, pad_bricks(): picked = jnp.take(facing, neighbour_ids[:, offset], axis=0)  33.3 us
  transfers between devices with their start and end apart: 10, of which 2 were waited for; matrix products, arithmetic and copies ran while one was open for 10% of the time, Pallas kernels for 0%

commit v1 on v0

--- a/solution.py
+++ b/solution.py
@@ -201,7 +201,7 @@
     grad_input = conv_transpose(padded_grad, w_sub, EDGE) * live
     grad_features = grad_input.reshape(bricks, channels, voxels).astype(jnp.bfloat16)
     sub_local = conv_weights(padded_input, grad_pre, EDGE)
-    grad_sub, grad_down = lax.psum((sub_local, down_local), ("gx", "yz"))
+    grad_sub, grad_down = lax.psum(lax.psum((sub_local, down_local), "yz"), "gx")
     return (coarse, grad_features, grad_sub, grad_down)
 
 

time: 815 us -> 845 us (1.037)
  waiting for transfers between devices: 149 us -> 177 us
    psum x1 -> x2, waiting for transfers between devices: 133 us -> 160 us  [the longest x1 90.7 us: on_device(): lax.psum(lax.psum((sub_local, down_local), 'yz'), 'gx')]
  transfers between devices with their start and end apart: 10 -> 11, of which waited for: 2 -> 3; matrix products, arithmetic and copies ran while one was open for 10% -> 10% of each run, Pallas kernels for 0% -> 0%
where the time goes in v1:
time: 845 us; the launch traced here: 836 us
  matrix products  260 us (31%)
  local copies, waits for them, and re-layouts  184 us (22%)
  waiting for transfers between devices  177 us (21%)
  other arithmetic  113 us (13%)
  blocking collectives  55.4 us (7%)
  starting transfers between devices  31.1 us (4%)
  between operations  16.4 us (2%)
    dot_general x27, matrix products, conv_forward(): jnp.einsum('oi,bixyz->boxyz', weights[offset], window, preferred_element_...  110 us
    dot_general x27, matrix products, conv_transpose(): jnp.einsum('oi,boxyz->bixyz', weights[offset], window, preferred_element_...  106 us
    psum x1, waiting for transfers between devices, on_device(): lax.psum(lax.psum((sub_local, down_local), 'yz'), 'gx')  90.7 us
    psum x1, waiting for transfers between devices, on_device(): lax.psum((sub_local, down_local), 'yz')  69.4 us
    gather x54, local copies, waits for them, and re-layouts, pad_bricks(): picked = jnp.take(facing, neighbour_ids[:, offset], axis=0)  63.4 us
    all_to_all x1, blocking collectives, on_device(): lax.all_to_all(outgoing, 'yz', split_axis=0, concat_axis=0, tiled=True)  55.4 us
    dot_general x27, matrix products, conv_weights(): jnp.einsum('boxyz,bixyz->oi', grads, window, preferred_element_type=jnp.f...  39 us
    scatter x52, other arithmetic, pad_bricks(): padded = padded.at[:, :, spans[0][1], spans[1][1], spans[2][1]].set(picked)  35.7 us
  transfers between devices with their start and end apart: 11, of which 3 were waited for; matrix products, arithmetic and copies ran while one was open for 10% of the time, Pallas kernels for 0%

profile of v1, /device:TPU:0, one launch (start us, length us, event | category | flops | bytes accessed | tf_op | source)
XLA Modules:
  0.0 836.0 jit_solution(5754169163693725641)
XLA Ops:
  13.5 6.5 collective-permute-start
  38.3 3.1 pad_maximum_fusion.2
  42.7 4.5 collective-permute-start.2
  47.9 3.3 copy.305
  66.5 6.2 pad_maximum_fusion
  72.7 12.1 %copy.306 = bf16[3,3,8,96,512]{3,2,1,0,4:T(8,128)(2,1)} copy(bf16[3,3,8,96,512]{4,3,2,1,0:T(8,128)(2,1)} %pad_maximum_fusion) | data formatting | bytes 14155776 | tf_op jit(solution)/shard_map/concatenate | solution.py:18
  84.8 8.6 %maximum_maximum_fusion = bf16[85,96,8,8,8]{1,0,4,3,2:T(8,128)(2,1)S(1)} fusion(bf16[72,96,8,8,8]{1,0,4,3,2:T(8,128)(2,1)} %bitcast.1018, bf16[12,96,8,8,8]{1,0,4,3,2:T(8,128)(2,1)S(1)} %bitcast.1024, bf16[85]{0:T(256)(128)(2,1)S(1)} %copy-done.94), kind=kLoop, calls=%fused_computation.57 | loop fusion | flops 25067520 | bytes 16613546 | tf_op jit(solution)/shard_map/concatenate | solution.py:139
  95.0 6.4 copy.325
  144.0 5.1 gather_fusion.15
  170.6 4.2 fusion.66
  184.3 4.5 fusion.281
  207.9 3.1 fusion.313
  257.4 37.2 %multiply_convert_fusion.1 = (bf16[12,96,8,8,8]{1,0,4,3,2:T(8,128)(2,1)S(1)}, f32[12,96,8,8,8]{1,0,4,3,2:T(8,128)}) fusion(f32[12,8,8,8]{0,3,2,1:T(8,128)S(1)} %bitcast.1029, bf16[12,96,10,10,10]{1,0,4,3,2:T(8,128)(2,1)} %constant_dynamic-update-slice_fusion.7, bf16[27,96,96]{2,1,0:T(8,128)(2,1)} %param.141, f32[12,8,8,8,96]{4,0,3,2,1:T(8,128)} %fusion.281, ...), kind=kOutput, calls=%fused_computation.88 | convolution fusion | flops 132120576 | bytes 116736000 | tf_op jit(solution)/shard_map/oi,bixyz->boxyz/dot_general | solution.py:64
  305.3 55.4 %all_to_all.10 = bf16[8,192,512]{2,1,0:T(8,128)(2,1)S(1)} all-to-all(bf16[8,192,512]{2,1,0:T(8,128)(2,1)} %copy.349), channel_id=1, replica_groups=mesh['gx'=4,'yz'=8] {'yz'}, dimensions={0} | all-to-all | bytes 3145728 | tf_op jit(solution)/shard_map/all_to_all | solution.py:180
  360.7 3.2 fusion.10
  363.9 4.3 all-to-all-start.1
  368.2 4.2 copy.395
  372.4 16.8 %all-to-all-done.1 = bf16[8,192,512]{2,1,0:T(8,128)(2,1)} async-done(((bf16[8,192,512]{2,1,0:T(8,128)(2,1)}), bf16[8,192,512]{2,1,0:T(8,128)(2,1)}, u32[]{:S(2)}, u32[]{:S(2)}) %all-to-all-start.1) | async-done | bytes 1572896 | tf_op jit(solution)/shard_map/all_to_all | solution.py:183
  389.2 3.2 copy.350
  392.4 3.5 copy.351
  396.0 3.6 reshape.2536
  413.1 5.9 collective-permute-start.4
  464.4 4.5 collective-permute-start.6
  468.9 69.4 %all-reduce.7.cloned.1.call-done = (f32[27,96,96]{2,1,0:T(8,128)}, f32[8,192,96]{1,0,2:T(8,128)}) async-done(((f32[27,96,96]{2,1,0:T(8,128)}, f32[8,192,96]{1,0,2:T(8,128)}), (f32[27,96,96]{2,1,0:T(8,128)}, f32[8,192,96]{1,0,2:T(8,128)})) %all-reduce.7.cloned.1.call-update) | async-done | bytes 1585168 | tf_op jit(solution)/shard_map/psum | solution.py:204
  538.3 90.7 %all-reduce.9.cloned.1.call-done = (f32[27,96,96]{2,1,0:T(8,128)}, f32[8,192,96]{1,0,2:T(8,128)}) async-done(((f32[27,96,96]{2,1,0:T(8,128)}, f32[8,192,96]{1,0,2:T(8,128)}), (f32[27,96,96]{2,1,0:T(8,128)}, f32[8,192,96]{1,0,2:T(8,128)})) %all-reduce.9.cloned.1.call-update) | async-done | bytes 1585168 | tf_op jit(solution)/shard_map/psum | solution.py:204
  631.4 6.2 pad_maximum_fusion.1
  637.7 12.1 %copy.460 = bf16[3,3,8,96,512]{3,2,1,0,4:T(8,128)(2,1)} copy(bf16[3,3,8,96,512]{4,3,2,1,0:T(8,128)(2,1)} %pad_maximum_fusion.1) | data formatting | bytes 14155776 | tf_op jit(solution)/shard_map/concatenate | solution.py:139
  649.7 8.6 %maximum_maximum_fusion.1 = bf16[85,96,8,8,8]{1,0,4,3,2:T(8,128)(2,1)S(1)} fusion(bf16[72,96,8,8,8]{1,0,4,3,2:T(8,128)(2,1)} %bitcast.1017, bf16[12,96,8,8,8]{1,0,4,3,2:T(8,128)(2,1)S(1)} %multiply_convert_fusion, bf16[85]{0:T(256)(128)(2,1)S(1)} %copy-done.95), kind=kLoop, calls=%fused_computation.58 | loop fusion | flops 25067520 | bytes 16613546 | tf_op jit(solution)/shard_map/concatenate | solution.py:139
  664.4 6.3 copy.375
  696.2 5.1 gather_fusion.43
  717.3 3.1 fusion.279
  788.5 35.2 %fusion.1 = bf16[12,96,8,8,8]{1,0,4,3,2:T(8,128)(2,1)S(1)} fusion(f32[12,8,8,8,96]{4,0,3,2,1:T(8,128)} %fusion.279, f32[12,8,8,8,96]{4,0,3,2,1:T(8,128)} %fusion.283, f32[12,8,8,8,96]{4,0,3,2,1:T(8,128)} %fusion.287, f32[12,8,8,8,96]{4,0,3,2,1:T(8,128)} %fusion.291, f32[12,8,8,8,96]{4,0,3,2,1:T(8,128)} %fusion.295, f32[12,8,8,8,96]{4,0,3,2,1:T(8,128)} %fusion.299, ...), kind=kOutput, calls=%fused_computation.66 | convolution fusion | flops 129761280 | bytes 114376704 | tf_op jit(solution)/shard_map/oi,boxyz->bixyz/dot_general | solution.py:82
  (538 shorter events, 373.7 us)
Async XLA Ops:
  7.2 289.4 %copy-start = (bf16[8,192,96]{2,1,0:T(8,128)(2,1)S(1)}, bf16[8,192,96]{2,1,0:T(8,128)(2,1)}, u32[]{:S(2)}) copy-start(bf16[8,192,96]{2,1,0:T(8,128)(2,1)} %param.142) | copy-start | bytes 884740
  7.9 33.5 %copy-start.96 = (pred[8]{0:T(512)(128)(4,1)}, pred[8]{0:T(512)(128)(4,1)S(1)}, u32[]{:S(2)}) copy-start(pred[8]{0:T(512)(128)(4,1)S(1)} %compare_and_fusion.27) | copy-start | bytes 28
  8.6 32.8 %copy-start.31 = (s32[1024]{0:T(1024)}, s32[1024]{0:T(1024)S(1)}, u32[]{:S(2)}) copy-start(s32[1024]{0:T(1024)S(1)} %pad_clamp_fusion.28) | copy-start | bytes 12292
  11.4 30.0 %copy-start.8 = (bf16[12,96,512]{2,1,0:T(8,128)(2,1)}, bf16[12,96,512]{2,1,0:T(8,128)(2,1)S(1)}, u32[]{:S(2)}) copy-start(bf16[12,96,512]{2,1,0:T(8,128)(2,1)S(1)} %broadcast_multiply_fusion) | copy-start | bytes 3538948
  12.2 26.1 %collective-permute-start.1 = (bf16[1,1,8,96,512]{4,3,2,1,0:T(8,128)(2,1)S(1)}, bf16[1,1,8,96,512]{4,3,2,1,0:T(8,128)(2,1)S(1)}, u32[]{:S(2)}, u32[]{:S(2)}) collective-permute-start(bf16[1,1,8,96,512]{4,3,2,1,0:T(8,128)(2,1)S(1)} %select_bitcast_fusion.1), channel_id=1, source_target_pairs={{8,0},{16,8},{24,16},{9,1},{17,9},{25,17},{10,2},{18,10},{26,18},{... | collective-permute-start | bytes 2359304 | tf_op jit(solution)/shard_map/ppermute | solution.py:17
  13.5 24.8 %collective-permute-start = (bf16[1,1,8,96,512]{4,3,2,1,0:T(8,128)(2,1)S(1)}, bf16[1,1,8,96,512]{4,3,2,1,0:T(8,128)(2,1)}, u32[]{:S(2)}, u32[]{:S(2)}) collective-permute-start(bf16[1,1,8,96,512]{4,3,2,1,0:T(8,128)(2,1)S(1)} %select_bitcast_fusion.1), channel_id=1, source_target_pairs={{0,8},{8,16},{16,24},{1,9},{9,17},{17,25},{2,10},{10,18},{18,26},{... | collective-permute-start | bytes 2359304 | tf_op jit(solution)/shard_map/ppermute | solution.py:16
  20.3 26.9 %copy-start.50 = (s32[12]{0:T(128)}, s32[12]{0:T(128)S(1)}, u32[]{:S(2)}) copy-start(s32[12]{0:T(128)S(1)} %get-tuple-element.700) | copy-start | bytes 148
  20.3 26.9 %copy-start.68 = (s32[12]{0:T(128)}, s32[12]{0:T(128)S(1)}, u32[]{:S(2)}) copy-start(s32[12]{0:T(128)S(1)} %get-tuple-element.699) | copy-start | bytes 148
  25.2 87.7 %copy-start.27 = (s32[1024]{0:T(1024)}, s32[1024]{0:T(1024)S(1)}, u32[]{:S(2)}) copy-start(s32[1024]{0:T(1024)S(1)} %pad_clamp_fusion.27) | copy-start | bytes 12292
  30.0 88.1 %copy-start.28 = (s32[1024]{0:T(1024)}, s32[1024]{0:T(1024)S(1)}, u32[]{:S(2)}) copy-start(s32[1024]{0:T(1024)S(1)} %pad_clamp_fusion.9) | copy-start | bytes 12292
  30.0 87.5 %copy-start.29 = (s32[1024]{0:T(1024)}, s32[1024]{0:T(1024)S(1)}, u32[]{:S(2)}) copy-start(s32[1024]{0:T(1024)S(1)} %pad_clamp_fusion.7) | copy-start | bytes 12292
  30.7 86.2 %copy-start.30 = (s32[1024]{0:T(1024)}, s32[1024]{0:T(1024)S(1)}, u32[]{:S(2)}) copy-start(s32[1024]{0:T(1024)S(1)} %pad_clamp_fusion.3) | copy-start | bytes 12292
  41.4 25.0 %collective-permute-start.3 = (bf16[3,1,8,96,512]{4,3,2,1,0:T(8,128)(2,1)}, bf16[3,1,8,96,512]{4,3,2,1,0:T(8,128)(2,1)}, u32[]{:S(2)}, u32[]{:S(2)}) collective-permute-start(bf16[3,1,8,96,512]{4,3,2,1,0:T(8,128)(2,1)} %pad_maximum_fusion.2), channel_id=1, source_target_pairs={{1,0},{2,1},{3,2},{4,3},{5,4},{6,5},{7,6},{9,8},{10,9},{11,10},{12... | collective-permute-start | bytes 7077896 | tf_op jit(solution)/shard_map/ppermute | solution.py:17
  42.7 23.7 %collective-permute-start.2 = (bf16[3,1,8,96,512]{4,3,2,1,0:T(8,128)(2,1)}, bf16[3,1,8,96,512]{4,3,2,1,0:T(8,128)(2,1)}, u32[]{:S(2)}, u32[]{:S(2)}) collective-permute-start(bf16[3,1,8,96,512]{4,3,2,1,0:T(8,128)(2,1)} %pad_maximum_fusion.2), channel_id=1, source_target_pairs={{0,1},{1,2},{2,3},{3,4},{4,5},{5,6},{6,7},{8,9},{9,10},{10,11},{11... | collective-permute-start | bytes 7077896 | tf_op jit(solution)/shard_map/ppermute | solution.py:16
  52.1 350.5 %copy-start.12 = (f32[12,512]{0,1:T(8,128)}, f32[12,512]{0,1:T(8,128)S(1)}, u32[]{:S(2)}) copy-start(f32[12,512]{0,1:T(8,128)S(1)} %copy.457) | copy-start | bytes 73732
  153.4 26.5 %copy-start.36 = (pred[12]{0:T(512)(128)(4,1)S(1)}, pred[12]{0:T(512)(128)(4,1)}, u32[]{:S(2)}) copy-start(pred[12]{0:T(512)(128)(4,1)} %get-tuple-element.805) | copy-start | bytes 40
  153.4 27.3 %copy-start.81 = (pred[12]{0:T(512)(128)(4,1)S(1)}, pred[12]{0:T(512)(128)(4,1)}, u32[]{:S(2)}) copy-start(pred[12]{0:T(512)(128)(4,1)} %get-tuple-element.804) | copy-start | bytes 40
  153.4 28.1 %copy-start.34 = (pred[12]{0:T(512)(128)(4,1)S(1)}, pred[12]{0:T(512)(128)(4,1)}, u32[]{:S(2)}) copy-start(pred[12]{0:T(512)(128)(4,1)} %get-tuple-element.803) | copy-start | bytes 40
  153.4 28.8 %copy-start.72 = (pred[12]{0:T(512)(128)(4,1)S(1)}, pred[12]{0:T(512)(128)(4,1)}, u32[]{:S(2)}) copy-start(pred[12]{0:T(512)(128)(4,1)} %get-tuple-element.802) | copy-start | bytes 40
  153.4 29.5 %copy-start.32 = (pred[12]{0:T(512)(128)(4,1)S(1)}, pred[12]{0:T(512)(128)(4,1)}, u32[]{:S(2)}) copy-start(pred[12]{0:T(512)(128)(4,1)} %get-tuple-element.801) | copy-start | bytes 40
  153.4 30.2 %copy-start.70 = (pred[12]{0:T(512)(128)(4,1)S(1)}, pred[12]{0:T(512)(128)(4,1)}, u32[]{:S(2)}) copy-start(pred[12]{0:T(512)(128)(4,1)} %get-tuple-element.800) | copy-start | bytes 40
  153.4 30.8 %copy-start.16 = (bf16[27,96,96]{2,1,0:T(8,128)(2,1)S(1)}, bf16[27,96,96]{2,1,0:T(8,128)(2,1)}, u32[]{:S(2)}) copy-start(bf16[27,96,96]{2,1,0:T(8,128)(2,1)} %param.141) | copy-start | bytes 1492996
  305.3 55.4 %copy-start.21 = (bf16[8,192,512]{2,1,0:T(8,128)(2,1)S(1)}, bf16[8,192,512]{2,1,0:T(8,128)(2,1)}, u32[]{:S(2)}) copy-start(bf16[8,192,512]{2,1,0:T(8,128)(2,1)} %param.143) | copy-start | bytes 4718596
  363.9 25.4 %all-to-all-start.1 = ((bf16[8,192,512]{2,1,0:T(8,128)(2,1)}), bf16[8,192,512]{2,1,0:T(8,128)(2,1)}, u32[]{:S(2)}, u32[]{:S(2)}) async-start(bf16[8,192,512]{2,1,0:T(8,128)(2,1)} %get-tuple-element.764), calls=%async_computation.1 | async-start | bytes 3145728 | tf_op jit(solution)/shard_map/all_to_all | solution.py:183
  368.2 170.1 %all-reduce.7.cloned.1.call-start = ((), (), s32[]{:S(2)}) async-start(), calls=%async_computation.2 | async-start | bytes 4227072 | tf_op jit(solution)/shard_map/psum | solution.py:204
  411.5 48.6 %collective-permute-start.5 = (bf16[1,1,8,96,512]{4,3,2,1,0:T(8,128)(2,1)S(1)}, bf16[1,1,8,96,512]{4,3,2,1,0:T(8,128)(2,1)}, u32[]{:S(2)}, u32[]{:S(2)}) collective-permute-start(bf16[1,1,8,96,512]{4,3,2,1,0:T(8,128)(2,1)S(1)} %select_bitcast_fusion), channel_id=1, source_target_pairs={{8,0},{16,8},{24,16},{9,1},{17,9},{25,17},{10,2},{18,10},{26,18},{... | collective-permute-start | bytes 2359304 | tf_op jit(solution)/shard_map/ppermute | solution.py:17
  413.1 47.0 %collective-permute-start.4 = (bf16[1,1,8,96,512]{4,3,2,1,0:T(8,128)(2,1)S(1)}, bf16[1,1,8,96,512]{4,3,2,1,0:T(8,128)(2,1)}, u32[]{:S(2)}, u32[]{:S(2)}) collective-permute-start(bf16[1,1,8,96,512]{4,3,2,1,0:T(8,128)(2,1)S(1)} %select_bitcast_fusion), channel_id=1, source_target_pairs={{0,8},{8,16},{16,24},{1,9},{9,17},{17,25},{2,10},{10,18},{18,26},{... | collective-permute-start | bytes 2359304 | tf_op jit(solution)/shard_map/ppermute | solution.py:16
  460.0 169.1 %all-reduce.9.cloned.1.call-start = ((), (), s32[]{:S(2)}) async-start(), calls=%async_computation.3 | async-start | bytes 4227072 | tf_op jit(solution)/shard_map/psum | solution.py:204
  463.1 168.3 %collective-permute-start.7 = (bf16[3,1,8,96,512]{4,3,2,1,0:T(8,128)(2,1)}, bf16[3,1,8,96,512]{4,3,2,1,0:T(8,128)(2,1)}, u32[]{:S(2)}, u32[]{:S(2)}) collective-permute-start(bf16[3,1,8,96,512]{4,3,2,1,0:T(8,128)(2,1)} %pad_maximum_fusion.3), channel_id=1, source_target_pairs={{1,0},{2,1},{3,2},{4,3},{5,4},{6,5},{7,6},{9,8},{10,9},{11,10},{12... | collective-permute-start | bytes 7077896 | tf_op jit(solution)/shard_map/ppermute | solution.py:17
  464.4 167.0 %collective-permute-start.6 = (bf16[3,1,8,96,512]{4,3,2,1,0:T(8,128)(2,1)}, bf16[3,1,8,96,512]{4,3,2,1,0:T(8,128)(2,1)}, u32[]{:S(2)}, u32[]{:S(2)}) collective-permute-start(bf16[3,1,8,96,512]{4,3,2,1,0:T(8,128)(2,1)} %pad_maximum_fusion.3), channel_id=1, source_target_pairs={{0,1},{1,2},{2,3},{3,4},{4,5},{5,6},{6,7},{8,9},{9,10},{10,11},{11... | collective-permute-start | bytes 7077896 | tf_op jit(solution)/shard_map/ppermute | solution.py:16
  717.3 68.5 %copy-start.4 = (bf16[12,96,10,10,10]{1,0,4,3,2:T(8,128)(2,1)}, bf16[12,96,10,10,10]{1,0,4,3,2:T(8,128)(2,1)S(1)}, u32[]{:S(2)}) copy-start(bf16[12,96,10,10,10]{1,0,4,3,2:T(8,128)(2,1)S(1)} %constant_dynamic-update-slice_fusion) | copy-start | bytes 6912004
  788.5 40.2 %copy-start.1 = (bf16[8,192,96]{2,1,0:T(8,128)(2,1)S(1)}, bf16[8,192,96]{2,1,0:T(8,128)(2,1)}, u32[]{:S(2)}) copy-start(bf16[8,192,96]{2,1,0:T(8,128)(2,1)} %param.142) | copy-start | bytes 884740
  (79 other events, 902.0 us)
Sparse Core Ops, SparseCore 0:
  460.1 78.1 all-reduce.6
  540.8 88.2 all-reduce.8
